TPU v7x, 32 devices: a whole 2x2x4 slice. The times are simulated.
32 devices in a mesh: rep: 2 (over x), dp: 4 (over y, core), ctx: 4 (over z).
Axes of the slice: x: 2, y: 2, z: 4, core: 2. Of those that a mesh axis runs over, the one named last changes fastest.
Arguments:
- frames: bfloat16 [8, 512, 1024], P(('rep', 'dp'), 'ctx'), may hold values from -24 to 24
- lengths: int32 [8], P(('rep', 'dp')), may hold values from 64 to 512, as said below
- cotangent: bfloat16 [8, 512, 1024], P(('rep', 'dp'), 'ctx'), may hold values from -6 to 6
- w_query: bfloat16 [1024, 512], P('dp'), may hold values from -0.5 to 0.5
- w_key: bfloat16 [1024, 512], P('dp'), may hold values from -0.5 to 0.5
- w_value: bfloat16 [1024, 512], P('dp'), may hold values from -0.1875 to 0.1875
- w_out: bfloat16 [512, 1024], P('dp'), may hold values from -0.25 to 0.25
Outputs:
- attended: bfloat16 [8, 512, 1024], P(('rep', 'dp'), 'ctx')
- grad_frames: bfloat16 [8, 512, 1024], P(('rep', 'dp'), 'ctx')
- grad_out: float32 [512, 1024], P('dp')
Inputs may be any that keep to these rules, and one draw needn't show every extreme that they name: `lengths`: number of real frames of each meeting; one meeting of every draw has all 512 frames real.
All inputs are finite; a program needn't handle non-finite values.
Results may differ from a plain program's by a relative error of at most 0.025.
The roundings to bfloat16 on the way count: a program that leaves them out, or rounds other values in their place, can miss the bound.
Values may be sent and summed in bfloat16 or wider, within the bound.
A program may use at most 64 MiB of HBM per device.

v0:
```python
import math
import jax
import jax.numpy as jnp
from jax import lax
from jax.sharding import PartitionSpec as P

HEAD = 128
MASKED_SCORE = -1e30


def head_split(matrix, head_count):
    return matrix.reshape(matrix.shape[0], head_count, matrix.shape[1] // head_count)


def forward_step(carry, key_part, value_part, offset, query_heads, length, score_scale):
    head_count = query_heads.shape[1]
    amount = key_part.shape[0]
    maxima, totals, accumulated = carry
    key_heads = head_split(key_part, head_count)
    value_heads = head_split(value_part, head_count)
    scores = (
        jnp.einsum("rhe,nhe->hrn", query_heads, key_heads, preferred_element_type=jnp.float32)
        * score_scale
    )
    usable = offset + jnp.arange(amount) < length
    scores = jnp.where(usable[None, None, :], scores, MASKED_SCORE)
    new_maxima = jnp.maximum(maxima, jnp.max(scores, axis=2))
    factor = jnp.exp(maxima - new_maxima)
    exponent = jnp.where(usable[None, None, :], jnp.exp(scores - new_maxima[:, :, None]), 0.0)
    totals = totals * factor + jnp.sum(exponent, axis=2)
    mixed = jnp.einsum(
        "hrn,nhe->hre",
        exponent.astype(jnp.bfloat16),
        value_heads,
        preferred_element_type=jnp.float32,
    )
    accumulated = accumulated * factor[:, :, None] + mixed
    return (new_maxima, totals, accumulated)


def query_step(
    grad_accum,
    key_part,
    value_part,
    offset,
    query_heads,
    context_heads,
    logsum,
    deltas,
    length,
    score_scale,
):
    head_count = query_heads.shape[1]
    amount = key_part.shape[0]
    key_heads = head_split(key_part, head_count)
    value_heads = head_split(value_part, head_count)
    scores = (
        jnp.einsum("rhe,nhe->hrn", query_heads, key_heads, preferred_element_type=jnp.float32)
        * score_scale
    )
    usable = offset + jnp.arange(amount) < length
    attention = jnp.where(usable[None, None, :], jnp.exp(scores - logsum[:, :, None]), 0.0)
    grad_prob = jnp.einsum(
        "rhe,nhe->hrn", context_heads, value_heads, preferred_element_type=jnp.float32
    )
    grad_score = (attention * (grad_prob - deltas[:, :, None])).astype(jnp.bfloat16)
    added = jnp.einsum("hrn,nhe->rhe", grad_score, key_heads, preferred_element_type=jnp.float32)
    return grad_accum + added * score_scale


def key_step(
    query_part,
    context_part,
    all_logsum,
    all_deltas,
    key_heads,
    value_heads,
    key_usable,
    score_scale,
):
    head_count = key_heads.shape[1]
    query_heads = head_split(query_part, head_count)
    context_heads = head_split(context_part, head_count)
    scores = (
        jnp.einsum("rhe,nhe->hrn", query_heads, key_heads, preferred_element_type=jnp.float32)
        * score_scale
    )
    attention = jnp.where(key_usable[None, None, :], jnp.exp(scores - all_logsum[:, :, None]), 0.0)
    grad_value = jnp.einsum(
        "hrn,rhe->nhe",
        attention.astype(jnp.bfloat16),
        context_heads,
        preferred_element_type=jnp.float32,
    )
    grad_prob = jnp.einsum(
        "rhe,nhe->hrn", context_heads, value_heads, preferred_element_type=jnp.float32
    )
    grad_score = (attention * (grad_prob - all_deltas[:, :, None])).astype(jnp.bfloat16)
    added = jnp.einsum("hrn,rhe->nhe", grad_score, query_heads, preferred_element_type=jnp.float32)
    return (added * score_scale, grad_value)


def back_project(gradient, weight):
    return lax.dot_general(
        gradient, weight, (((1,), (1,)), ((), ())), preferred_element_type=jnp.float32
    )


def shards(frames, lengths, cotangent, w_query, w_key, w_value, w_out):
    full_query, full_key, full_value, full_out = (
        lax.all_gather(w_query, "dp", axis=0, tiled=True),
        lax.all_gather(w_key, "dp", axis=0, tiled=True),
        lax.all_gather(w_value, "dp", axis=0, tiled=True),
        lax.all_gather(w_out, "dp", axis=0, tiled=True),
    )
    inputs = frames[0]
    upstream = cotangent[0]
    length = lengths[0]
    row_count = inputs.shape[0]
    inner_width = full_query.shape[1]
    head_count = inner_width // HEAD
    score_scale = HEAD ** (-0.5)
    first_frame = lax.axis_index("ctx") * row_count
    row_usable = first_frame + jnp.arange(row_count) < length
    queries = jnp.dot(inputs, full_query, preferred_element_type=jnp.float32).astype(jnp.bfloat16)
    keys = jnp.dot(inputs, full_key, preferred_element_type=jnp.float32).astype(jnp.bfloat16)
    values = jnp.dot(inputs, full_value, preferred_element_type=jnp.float32).astype(jnp.bfloat16)
    query_heads = head_split(queries, head_count)
    key_heads = head_split(keys, head_count)
    value_heads = head_split(values, head_count)
    start_state = (
        jnp.full((head_count, row_count), MASKED_SCORE, jnp.float32),
        jnp.zeros((head_count, row_count), jnp.float32),
        jnp.zeros((head_count, row_count, HEAD), jnp.float32),
    )
    all_keys, all_values = (
        lax.all_gather(keys, "ctx", axis=0, tiled=True),
        lax.all_gather(values, "ctx", axis=0, tiled=True),
    )
    key_block = row_count * math.gcd(max(1, 512 // row_count), lax.axis_size("ctx"))
    block_count = all_keys.shape[0] // key_block
    key_blocks = all_keys.reshape(block_count, key_block, inner_width)
    value_blocks = all_values.reshape(block_count, key_block, inner_width)
    block_starts = jnp.arange(block_count, dtype=jnp.int32) * key_block

    def scan_forward(current, scan_item):
        return (
            forward_step(
                current, scan_item[0], scan_item[1], scan_item[2], query_heads, length, score_scale
            ),
            None,
        )

    softmax_state, unused = lax.scan(
        scan_forward, start_state, (key_blocks, value_blocks, block_starts)
    )
    maxima, totals, accumulated = softmax_state
    context = (
        (accumulated / totals[:, :, None])
        .transpose(1, 0, 2)
        .reshape(row_count, inner_width)
        .astype(jnp.bfloat16)
    )
    logsum = maxima + jnp.log(totals)
    attended = jnp.dot(context, full_out, preferred_element_type=jnp.float32)
    attended = jnp.where(row_usable[:, None], attended, 0.0).astype(jnp.bfloat16)
    masked_grad = jnp.where(row_usable[:, None], upstream, jnp.zeros_like(upstream))
    grad_context = back_project(masked_grad, full_out).astype(jnp.bfloat16)
    deltas = jnp.sum(
        (grad_context.astype(jnp.float32) * context.astype(jnp.float32)).reshape(
            row_count, head_count, HEAD
        ),
        axis=2,
    )
    context_heads = head_split(grad_context, head_count)
    delta_heads = deltas.T
    all_logsum, all_deltas = (
        lax.all_gather(logsum, "ctx", axis=1, tiled=True),
        lax.all_gather(delta_heads, "ctx", axis=1, tiled=True),
    )
    zero_grad = jnp.zeros((row_count, head_count, HEAD), jnp.float32)

    def scan_query(current, scan_item):
        return (
            query_step(
                current,
                scan_item[0],
                scan_item[1],
                scan_item[2],
                query_heads,
                context_heads,
                logsum,
                delta_heads,
                length,
                score_scale,
            ),
            None,
        )

    grad_query, unused = lax.scan(scan_query, zero_grad, (key_blocks, value_blocks, block_starts))
    grad_key, grad_value = key_step(
        lax.all_gather(queries, "ctx", axis=0, tiled=True),
        lax.all_gather(grad_context, "ctx", axis=0, tiled=True),
        all_logsum,
        all_deltas,
        key_heads,
        value_heads,
        row_usable,
        score_scale,
    )
    grad_query = grad_query.reshape(row_count, inner_width).astype(jnp.bfloat16)
    grad_key = grad_key.reshape(row_count, inner_width).astype(jnp.bfloat16)
    grad_value = grad_value.reshape(row_count, inner_width).astype(jnp.bfloat16)
    grad_input = (
        back_project(grad_query, full_query)
        + back_project(grad_key, full_key)
        + back_project(grad_value, full_value)
    )
    grad_frames = grad_input.astype(jnp.bfloat16)
    summed_grad = lax.psum(
        lax.dot_general(
            context, masked_grad, (((0,), (0,)), ((), ())), preferred_element_type=jnp.float32
        ),
        ("rep", "ctx"),
    )
    grad_out = lax.psum_scatter(summed_grad, "dp", scatter_dimension=0, tiled=True)
    return (attended[None], grad_frames[None], grad_out)


def solution(mesh):
    in_specs = (
        P(("rep", "dp"), "ctx", None),
        P(("rep", "dp")),
        P(("rep", "dp"), "ctx", None),
        P("dp", None),
        P("dp", None),
        P("dp", None),
        P("dp", None),
    )
    out_specs = (P(("rep", "dp"), "ctx", None), P(("rep", "dp"), "ctx", None), P("dp", None))
    return jax.shard_map(shards, mesh=mesh, in_specs=in_specs, out_specs=out_specs, check_vma=False)
```

profile of v0, /device:TPU:0, one launch (start us, length us, event | category | flops | bytes accessed | tf_op | source)
XLA Modules:
  0.0 236.2 jit_solution(8206433220303085801)
XLA Ops:
  7.2 0.7 all-gather.9.cloned.1.call-update
  7.9 0.0 all-gather.7.cloned.1.call-start
  8.0 0.7 all-gather.7.cloned.1.call-update
  8.7 0.0 all-gather.5.cloned.1.call-start
  8.7 0.7 all-gather.5.cloned.1.call-update
  9.4 0.0 all-gather.11.cloned.1.call-start
  9.4 0.5 all-gather.11.cloned.1.call-update
  10.0 0.0 reduce-scatter.2.cloned.1.call-start
  10.7 18.3 %all-gather.9.cloned.1.call-done = bf16[1024,512]{1,0:T(8,128)(2,1)} async-done(((bf16[256,512]{1,0:T(8,128)(2,1)}), bf16[1024,512]{1,0:T(8,128)(2,1)}) %all-gather.9.cloned.1.call-update) | async-done | bytes 1048592 | tf_op jit(solution)/shard_map/all_gather | solution.py:113
  29.0 1.5 convolution_convert_fusion.2
  30.6 16.1 %all_gather.34 = bf16[512,512]{1,0:T(8,128)(2,1)S(1)} all-gather(bf16[128,512]{1,0:T(8,128)(2,1)S(1)} %convolution_convert_fusion.2), channel_id=1, replica_groups=mesh['rep'=2,'dp'=4,'ctx'=4] {'ctx'}, dimensions={0}, use_global_device_ids=true | all-gather | bytes 655360 | tf_op jit(solution)/shard_map/all_gather | solution.py:138
  46.6 0.2 copy.33
  46.9 0.5 all-gather.7.cloned.1.call-done
  47.4 1.5 convolution_convert_fusion.3
  48.9 16.0 %all_gather.32 = bf16[512,512]{1,0:T(8,128)(2,1)S(1)} all-gather(bf16[128,512]{1,0:T(8,128)(2,1)S(1)} %convolution_convert_fusion.3), channel_id=1, replica_groups=mesh['rep'=2,'dp'=4,'ctx'=4] {'ctx'}, dimensions={0}, use_global_device_ids=true | all-gather | bytes 655360 | tf_op jit(solution)/shard_map/all_gather | solution.py:137
  64.9 0.2 copy.35
  65.1 0.5 all-gather.5.cloned.1.call-done
  65.7 1.5 convolution_convert_fusion.4
  67.2 0.4 select_reduce_fusion
  67.6 0.3 fusion.23
  68.0 0.4 fusion.19
  68.4 0.2 copy-done.5
  68.6 1.8 fusion.36
  70.4 0.0 all-reduce.2.cloned.1.call-start
  70.5 0.1 copy.22
  70.6 0.8 copy.34
  71.3 12.5 %all-gather.11.cloned.1.call-done = bf16[512,1024]{1,0:T(8,128)(2,1)} async-done(((bf16[128,1024]{1,0:T(8,128)(2,1)}), bf16[512,1024]{1,0:T(8,128)(2,1)}) %all-gather.11.cloned.1.call-update) | async-done | bytes 1048592 | tf_op jit(solution)/shard_map/all_gather | solution.py:114
  83.9 1.7 convert_multiply_fusion
  85.6 0.1 reshape.104
  85.7 0.2 reduce_sum.23
  85.9 0.6 copy.23
  86.5 16.1 %all_gather.36 = bf16[512,512]{1,0:T(8,128)(2,1)S(1)} all-gather(bf16[128,512]{1,0:T(8,128)(2,1)S(1)} %convolution_convert_fusion.4), channel_id=1, replica_groups=mesh['rep'=2,'dp'=4,'ctx'=4] {'ctx'}, dimensions={0}, use_global_device_ids=true | all-gather | bytes 655360 | tf_op jit(solution)/shard_map/all_gather | solution.py:202
  102.6 1.1 copy.36
  103.6 16.0 %all_gather.38 = bf16[512,512]{1,0:T(8,128)(2,1)S(1)} all-gather(bf16[128,512]{1,0:T(8,128)(2,1)S(1)} %get-tuple-element.50), channel_id=1, replica_groups=mesh['rep'=2,'dp'=4,'ctx'=4] {'ctx'}, dimensions={0}, use_global_device_ids=true | all-gather | bytes 655360 | tf_op jit(solution)/shard_map/all_gather | solution.py:203
  119.6 0.2 copy.37
  119.8 14.3 %all_gather.39 = f32[4,512]{0,1:T(8,128)S(1)} all-gather(f32[4,128]{0,1:T(8,128)S(1)} %bitcast.109), channel_id=1, replica_groups=mesh['rep'=2,'dp'=4,'ctx'=4] {'ctx'}, dimensions={1}, use_global_device_ids=true | all-gather | bytes 10240 | tf_op jit(solution)/shard_map/all_gather | solution.py:179
  134.1 0.1 copy.27
  134.2 11.9 %all_gather.37 = f32[4,512]{1,0:T(4,128)S(1)} all-gather(f32[4,128]{1,0:T(4,128)S(1)} %get-tuple-element.36), channel_id=1, replica_groups=mesh['rep'=2,'dp'=4,'ctx'=4] {'ctx'}, dimensions={1}, use_global_device_ids=true | all-gather | bytes 10240 | tf_op jit(solution)/shard_map/all_gather | solution.py:178
  146.1 1.6 fusion.3
  147.6 1.0 convolution_convert_fusion
  148.7 2.3 fusion.18
  151.0 2.7 %fusion.60 = f32[128,1024]{1,0:T(8,128)} fusion(bf16[128,512]{0,1:T(8,128)(2,1)} %bitcast.115, bf16[1024,512]{1,0:T(8,128)(2,1)} %all-gather.5.cloned.1.call-done), kind=kOutput, calls=%fused_computation.80 | convolution fusion | flops 134217728 | bytes 1703936 | tf_op jit(solution)/shard_map/dot_general | solution.py:104
  153.7 2.9 %fusion.17 = bf16[4,128,128]{2,1,0:T(8,128)(2,1)} fusion(bf16[512,4,128]{0,2,1:T(8,128)(2,1)} %bitcast.104, f32[4,512,128]{2,1,0:T(8,128)} %copy-done.4, bf16[512,4,128]{0,2,1:T(8,128)(2,1)S(1)} %bitcast.100, bf16[128,4,128]{0,2,1:T(8,128)(2,1)} %bitcast.111, f32[4,512]{1,0:T(4,128)S(1)} %copy.27), kind=kOutput, calls=%fused_computation.30 | convolution fusion | flops 135135232 | bytes 2367488 | tf_op jit(solution)/shard_map/hrn,rhe->nhe/dot_general | solution.py:99
  156.6 1.0 fusion.14
  157.6 1.6 convolution_add_fusion.1
  159.3 1.2 fusion.13
  160.4 67.1 %all-reduce.2.cloned.1.call-done = f32[128,1024]{1,0:T(8,128)} async-done(((f32[128,1024]{1,0:T(8,128)}), f32[128,1024]{1,0:T(8,128)}) %all-reduce.2.cloned.1.call-update) | async-done | bytes 524304 | tf_op jit(solution)/shard_map/psum | solution.py:220
  227.5 1.9 copy.58
  (30 shorter events, 0.2 us)
Async XLA Ops:
  7.2 21.9 %copy-start = (bf16[1,128,1024]{2,1,0:T(8,128)(2,1)S(1)}, bf16[1,128,1024]{2,1,0:T(8,128)(2,1)}, u32[]{:S(2)}) copy-start(bf16[1,128,1024]{2,1,0:T(8,128)(2,1)} %param.7) | copy-start | bytes 786436
  7.2 21.9 %all-gather.9.cloned.1.call-start = ((), (), s32[]{:S(2)}) async-start(), calls=%async_computation.3 | async-start | bytes 1310720 | tf_op jit(solution)/shard_map/all_gather | solution.py:113
  7.9 39.4 %all-gather.7.cloned.1.call-start = ((), (), s32[]{:S(2)}) async-start(), calls=%async_computation.2 | async-start | bytes 1310720 | tf_op jit(solution)/shard_map/all_gather | solution.py:112
  8.7 57.0 %all-gather.5.cloned.1.call-start = ((), (), s32[]{:S(2)}) async-start(), calls=%async_computation.1 | async-start | bytes 1310720 | tf_op jit(solution)/shard_map/all_gather | solution.py:111
  9.4 74.5 %all-gather.11.cloned.1.call-start = ((), (), s32[]{:S(2)}) async-start(), calls=%async_computation.4 | async-start | bytes 1310720 | tf_op jit(solution)/shard_map/all_gather | solution.py:114
  10.0 146.6 %reduce-scatter.2.cloned.1.call-start = ((), (), s32[]{:S(2)}) async-start(), calls=%async_computation.5 | async-start | bytes 2621440 | tf_op jit(solution)/shard_map/reduce_scatter | solution.py:226
  10.7 57.3 %copy-start.10 = (pred[512]{0:T(512)(128)(4,1)}, pred[512]{0:T(512)(128)(4,1)S(1)}, u32[]{:S(2)}) copy-start(pred[512]{0:T(512)(128)(4,1)S(1)} %iota_compare_fusion) | copy-start | bytes 1540
  46.9 21.1 %copy-start.6 = (bf16[512,512]{0,1:T(8,128)(2,1)}, bf16[512,512]{0,1:T(8,128)(2,1)S(1)}, u32[]{:S(2)}) copy-start(bf16[512,512]{0,1:T(8,128)(2,1)S(1)} %copy.33) | copy-start | bytes 1572868
  48.9 18.3 %copy-start.7 = (bf16[128,512]{1,0:T(8,128)(2,1)}, bf16[128,512]{1,0:T(8,128)(2,1)S(1)}, u32[]{:S(2)}) copy-start(bf16[128,512]{1,0:T(8,128)(2,1)S(1)} %convolution_convert_fusion.3) | copy-start | bytes 393220
  67.6 1.0 copy-start.5
  70.4 157.1 %all-reduce.2.cloned.1.call-start = ((), (), s32[]{:S(2)}) async-start(), calls=%async_computation.6 | async-start | bytes 1048576 | tf_op jit(solution)/shard_map/psum | solution.py:220
  85.6 34.3 %copy-start.8 = (bf16[128,512]{1,0:T(8,128)(2,1)}, bf16[128,512]{1,0:T(8,128)(2,1)S(1)}, u32[]{:S(2)}) copy-start(bf16[128,512]{1,0:T(8,128)(2,1)S(1)} %get-tuple-element.50) | copy-start | bytes 393220
  147.6 3.4 %copy-start.4 = (f32[4,512,128]{2,1,0:T(8,128)}, f32[4,512,128]{2,1,0:T(8,128)S(1)}, u32[]{:S(2)}) copy-start(f32[4,512,128]{2,1,0:T(8,128)S(1)} %fusion.3) | copy-start | bytes 3145732
  151.0 5.6 %copy-start.2 = (bf16[512,1024]{1,0:T(8,128)(2,1)S(1)}, bf16[512,1024]{1,0:T(8,128)(2,1)}, u32[]{:S(2)}) copy-start(bf16[512,1024]{1,0:T(8,128)(2,1)} %all-gather.11.cloned.1.call-done) | copy-start | bytes 3145732
  153.7 4.0 %copy-start.1 = (bf16[1024,512]{1,0:T(8,128)(2,1)S(1)}, bf16[1024,512]{1,0:T(8,128)(2,1)}, u32[]{:S(2)}) copy-start(bf16[1024,512]{1,0:T(8,128)(2,1)} %all-gather.7.cloned.1.call-done) | copy-start | bytes 3145732
  156.6 2.7 %copy-start.3 = (bf16[1024,512]{1,0:T(8,128)(2,1)S(1)}, bf16[1024,512]{1,0:T(8,128)(2,1)}, u32[]{:S(2)}) copy-start(bf16[1024,512]{1,0:T(8,128)(2,1)} %all-gather.9.cloned.1.call-done) | copy-start | bytes 3145732
  156.6 2.7 %copy-start.9 = (bf16[4,128,128]{2,1,0:T(8,128)(2,1)S(1)}, bf16[4,128,128]{2,1,0:T(8,128)(2,1)}, u32[]{:S(2)}) copy-start(bf16[4,128,128]{2,1,0:T(8,128)(2,1)} %convolution_convert_fusion) | copy-start | bytes 393220
Sparse Core Ops, SparseCore 0:
  9.6 19.4 all-gather.8
  30.6 16.7 all-gather.6
  48.9 16.7 all-gather.4
  67.1 16.7 all-gather.10
  86.2 31.4 reduce-scatter.1
  156.7 70.7 all-reduce.1
where the time goes:
time: 237 us; the launch traced here: 236 us
  waiting for transfers between devices  102 us (43%)
  blocking collectives  90.2 us (38%)
  matrix products  23.2 us (10%)
  between operations  15 us (6%)
  local copies, waits for them, and re-layouts  5.47 us (2%)
    psum x1, waiting for transfers between devices, shards(): lax.psum(lax.dot_general(context, masked_grad, (((0,), (0,)), ((), ())),...  67.1 us
    all_gather x1, waiting for transfers between devices, shards(): lax.all_gather(w_value, 'dp', axis=0, tiled=True)  18.3 us
    all_gather x1, blocking collectives, shards(): lax.all_gather(values, 'ctx', axis=0, tiled=True)  16.1 us
    all_gather x1, blocking collectives, shards(): lax.all_gather(queries, 'ctx', axis=0, tiled=True)  16.1 us
    all_gather x1, blocking collectives, shards(): lax.all_gather(keys, 'ctx', axis=0, tiled=True)  16 us
    all_gather x1, blocking collectives, shards(): lax.all_gather(grad_context, 'ctx', axis=0, tiled=True)  16 us
    all_gather x1, blocking collectives, shards(): lax.all_gather(delta_heads, 'ctx', axis=1, tiled=True)  14.3 us
    all_gather x1, waiting for transfers between devices, shards(): lax.all_gather(w_out, 'dp', axis=0, tiled=True)  12.5 us
  transfers between devices with their start and end apart: 6, of which 5 were waited for; matrix products, arithmetic and copies ran while one was open for 11% of the time, Pallas kernels for 0%

commit v1 on v0

--- a/solution.py
+++ b/solution.py
@@ -217,12 +217,11 @@
         + back_project(grad_value, full_value)
     )
     grad_frames = grad_input.astype(jnp.bfloat16)
-    summed_grad = lax.psum(
-        lax.dot_general(
-            context, masked_grad, (((0,), (0,)), ((), ())), preferred_element_type=jnp.float32
-        ),
-        ("rep", "ctx"),
-    )
+    block = lax.dot_general(
+        context, masked_grad, (((0,), (0,)), ((), ())), preferred_element_type=jnp.float32
+    )
+    pieces = lax.all_gather(block, ("rep", "ctx"))
+    summed_grad = jnp.sum(pieces, axis=0)
     grad_out = lax.psum_scatter(summed_grad, "dp", scatter_dimension=0, tiled=True)
     return (attended[None], grad_frames[None], grad_out)
 

time: 237 us -> 411 us (1.73)
  waiting for transfers between devices: 102 us -> 266 us
  other arithmetic: 0.59 us -> 9.94 us
    all_gather x0 -> x1, waiting for transfers between devices: none -> 228 us  [shards(): pieces = lax.all_gather(block, ('rep', 'ctx'))]
    psum x1 -> x0, waiting for transfers between devices: 67.1 us -> none  [shards(): lax.psum(lax.dot_general(context, masked_grad, (((0,), (0,)), ((), ())),...]
    all_gather x1, waiting for transfers between devices: 0.49 us -> 18.9 us  [shards(): lax.all_gather(w_key, 'dp', axis=0, tiled=True)]
    all_gather x1, waiting for transfers between devices: 12.5 us -> 0.01 us  [shards(): lax.all_gather(w_out, 'dp', axis=0, tiled=True)]
    reduce_sum x0 -> x1, other arithmetic: none -> 9.35 us  [shards(): summed_grad = jnp.sum(pieces, axis=0)]
  transfers between devices with their start and end apart: 6 -> 6, of which waited for: 5 -> 4; matrix products, arithmetic and copies ran while one was open for 11% -> 8% of each run, Pallas kernels for 0% -> 0%
where the time goes in v1:
time: 411 us; the launch traced here: 410 us
  waiting for transfers between devices  266 us (65%)
  blocking collectives  90.3 us (22%)
  matrix products  22 us (5%)
  between operations  15 us (4%)
  other arithmetic  9.94 us (2%)
  local copies, waits for them, and re-layouts  7.28 us (2%)
    all_gather x1, waiting for transfers between devices, shards(): pieces = lax.all_gather(block, ('rep', 'ctx'))  228 us
    all_gather x1, waiting for transfers between devices, shards(): lax.all_gather(w_key, 'dp', axis=0, tiled=True)  18.9 us
    all_gather x1, blocking collectives, shards(): lax.all_gather(grad_context, 'ctx', axis=0, tiled=True)  16.7 us
    all_gather x1, blocking collectives, shards(): lax.all_gather(values, 'ctx', axis=0, tiled=True)  16.1 us
    all_gather x1, blocking collectives, shards(): lax.all_gather(keys, 'ctx', axis=0, tiled=True)  16.1 us
    all_gather x1, waiting for transfers between devices, shards(): lax.all_gather(w_value, 'dp', axis=0, tiled=True)  16 us
    all_gather x1, blocking collectives, shards(): lax.all_gather(queries, 'ctx', axis=0, tiled=True)  15.4 us
    all_gather x1, blocking collectives, shards(): lax.all_gather(delta_heads, 'ctx', axis=1, tiled=True)  14.2 us
  transfers between devices with their start and end apart: 6, of which 4 were waited for; matrix products, arithmetic and copies ran while one was open for 8% of the time, Pallas kernels for 0%

profile of v1, /device:TPU:0, one launch (start us, length us, event | category | flops | bytes accessed | tf_op | source)
XLA Modules:
  0.0 410.2 jit_solution(10125585143240210003)
XLA Ops:
  7.2 0.7 all-gather.9.cloned.1.call-update
  7.9 0.0 all-gather.7.cloned.1.call-start
  8.0 0.7 all-gather.7.cloned.1.call-update
  8.7 0.0 all-gather.11.cloned.1.call-start
  8.7 0.7 all-gather.11.cloned.1.call-update
  9.4 0.0 all-gather.15.cloned.1.call-start
  10.1 18.9 %all-gather.9.cloned.1.call-done = bf16[1024,512]{1,0:T(8,128)(2,1)} async-done(((bf16[256,512]{1,0:T(8,128)(2,1)}), bf16[1024,512]{1,0:T(8,128)(2,1)}) %all-gather.9.cloned.1.call-update) | async-done | bytes 1048592 | tf_op jit(solution)/shard_map/all_gather | solution.py:112
  29.0 1.5 convolution_convert_fusion.3
  30.6 16.1 %all_gather.38 = bf16[512,512]{1,0:T(8,128)(2,1)S(1)} all-gather(bf16[128,512]{1,0:T(8,128)(2,1)S(1)} %convolution_convert_fusion.3), channel_id=1, replica_groups=mesh['rep'=2,'dp'=4,'ctx'=4] {'ctx'}, dimensions={0}, use_global_device_ids=true | all-gather | bytes 655360 | tf_op jit(solution)/shard_map/all_gather | solution.py:137
  46.6 0.2 copy.35
  46.9 0.5 all-gather.7.cloned.1.call-done
  47.3 1.5 convolution_convert_fusion.4
  48.9 0.4 select_reduce_fusion
  49.3 0.3 fusion.23
  49.7 16.0 %all-gather.11.cloned.1.call-done = bf16[1024,512]{1,0:T(8,128)(2,1)} async-done(((bf16[256,512]{1,0:T(8,128)(2,1)}), bf16[1024,512]{1,0:T(8,128)(2,1)}) %all-gather.11.cloned.1.call-update) | async-done | bytes 1048592 | tf_op jit(solution)/shard_map/all_gather | solution.py:113
  65.7 1.5 convolution_convert_fusion.2
  67.2 16.1 %all_gather.40 = bf16[512,512]{1,0:T(8,128)(2,1)S(1)} all-gather(bf16[128,512]{1,0:T(8,128)(2,1)S(1)} %convolution_convert_fusion.2), channel_id=1, replica_groups=mesh['rep'=2,'dp'=4,'ctx'=4] {'ctx'}, dimensions={0}, use_global_device_ids=true | all-gather | bytes 655360 | tf_op jit(solution)/shard_map/all_gather | solution.py:138
  83.3 1.0 copy.33
  84.3 1.4 fusion.19
  85.7 1.8 fusion.36
  87.6 0.0 all-gather.13.cloned.1.call-start
  87.7 0.5 all-gather.13.cloned.1.call-update
  88.2 0.0 reduce-scatter.2.cloned.1.call-start
  88.2 227.5 %all-gather.15.cloned.1.call-done = f32[4096,1024]{1,0:T(8,128)} async-done(((f32[512,1024]{1,0:T(8,128)}), f32[4096,1024]{1,0:T(8,128)}) %all-gather.15.cloned.1.call-update) | async-done | bytes 16777232 | tf_op jit(solution)/shard_map/all_gather | solution.py:223
  315.8 9.3 %reduce_sum.33 = f32[512,1024]{1,0:T(8,128)} reduce(f32[8,512,1024]{2,1,0:T(8,128)} %bitcast.100, f32[]{:T(128)} %constant.28.clone.1), dimensions={0}, to_apply=%region_3.4 | reduce | flops 3670016 | bytes 18874372 | tf_op jit(solution)/shard_map/reduce_sum | solution.py:224
  325.1 0.8 copy.34
  325.9 0.8 copy.22
  326.7 15.4 %all_gather.42 = bf16[512,512]{1,0:T(8,128)(2,1)S(1)} all-gather(bf16[128,512]{1,0:T(8,128)(2,1)S(1)} %convolution_convert_fusion.4), channel_id=1, replica_groups=mesh['rep'=2,'dp'=4,'ctx'=4] {'ctx'}, dimensions={0}, use_global_device_ids=true | all-gather | bytes 655360 | tf_op jit(solution)/shard_map/all_gather | solution.py:202
  342.1 1.0 copy.36
  343.1 2.5 convert_multiply_fusion
  345.6 0.1 reshape.104
  345.7 0.2 reduce_sum.32
  345.9 0.7 copy.23
  346.6 14.2 %all_gather.45 = f32[4,512]{0,1:T(8,128)S(1)} all-gather(f32[4,128]{0,1:T(8,128)S(1)} %bitcast.111), channel_id=1, replica_groups=mesh['rep'=2,'dp'=4,'ctx'=4] {'ctx'}, dimensions={1}, use_global_device_ids=true | all-gather | bytes 10240 | tf_op jit(solution)/shard_map/all_gather | solution.py:179
  360.8 0.1 copy.27
  360.9 16.7 %all_gather.44 = bf16[512,512]{1,0:T(8,128)(2,1)} all-gather(bf16[128,512]{1,0:T(8,128)(2,1)} %get-tuple-element.50), channel_id=1, replica_groups=mesh['rep'=2,'dp'=4,'ctx'=4] {'ctx'}, dimensions={0}, use_global_device_ids=true | all-gather | bytes 655360 | tf_op jit(solution)/shard_map/all_gather | solution.py:203
  377.6 1.3 copy.37
  378.8 11.9 %all_gather.43 = f32[4,512]{1,0:T(4,128)S(1)} all-gather(f32[4,128]{1,0:T(4,128)S(1)} %get-tuple-element.36), channel_id=1, replica_groups=mesh['rep'=2,'dp'=4,'ctx'=4] {'ctx'}, dimensions={1}, use_global_device_ids=true | all-gather | bytes 10240 | tf_op jit(solution)/shard_map/all_gather | solution.py:178
  390.7 1.0 fusion.14
  391.7 1.6 fusion.3
  393.3 1.0 copy-done.5
  394.3 1.0 convolution_convert_fusion
  395.3 2.3 fusion.18
  397.6 1.5 fusion.60
  399.1 2.2 fusion.17
  401.3 0.5 convolution_add_fusion.1
  401.8 0.4 copy-done.9
  402.2 1.2 fusion.13
  (30 shorter events, 0.2 us)
Async XLA Ops:
  7.2 21.9 %copy-start = (bf16[1,128,1024]{2,1,0:T(8,128)(2,1)S(1)}, bf16[1,128,1024]{2,1,0:T(8,128)(2,1)}, u32[]{:S(2)}) copy-start(bf16[1,128,1024]{2,1,0:T(8,128)(2,1)} %param.7) | copy-start | bytes 786436
  7.2 21.9 %all-gather.9.cloned.1.call-start = ((), (), s32[]{:S(2)}) async-start(), calls=%async_computation.2 | async-start | bytes 1310720 | tf_op jit(solution)/shard_map/all_gather | solution.py:112
  7.9 39.4 %all-gather.7.cloned.1.call-start = ((), (), s32[]{:S(2)}) async-start(), calls=%async_computation.1 | async-start | bytes 1310720 | tf_op jit(solution)/shard_map/all_gather | solution.py:111
  8.7 57.0 %all-gather.11.cloned.1.call-start = ((), (), s32[]{:S(2)}) async-start(), calls=%async_computation.3 | async-start | bytes 1310720 | tf_op jit(solution)/shard_map/all_gather | solution.py:113
  9.4 306.4 %all-gather.15.cloned.1.call-start = ((), (), s32[]{:S(2)}) async-start(), calls=%async_computation.6 | async-start | bytes 18874368 | tf_op jit(solution)/shard_map/all_gather | solution.py:223
  10.1 74.2 %copy-start.10 = (pred[512]{0:T(512)(128)(4,1)}, pred[512]{0:T(512)(128)(4,1)S(1)}, u32[]{:S(2)}) copy-start(pred[512]{0:T(512)(128)(4,1)S(1)} %iota_compare_fusion) | copy-start | bytes 1540
  30.6 18.3 %copy-start.7 = (bf16[128,512]{1,0:T(8,128)(2,1)}, bf16[128,512]{1,0:T(8,128)(2,1)S(1)}, u32[]{:S(2)}) copy-start(bf16[128,512]{1,0:T(8,128)(2,1)S(1)} %convolution_convert_fusion.3) | copy-start | bytes 393220
  83.3 2.5 copy-start.6
  87.6 255.5 %all-gather.13.cloned.1.call-start = ((), (), s32[]{:S(2)}) async-start(), calls=%async_computation.4 | async-start | bytes 1310720 | tf_op jit(solution)/shard_map/all_gather | solution.py:114
  88.2 315.2 %reduce-scatter.2.cloned.1.call-start = ((), (), s32[]{:S(2)}) async-start(), calls=%async_computation.5 | async-start | bytes 2621440 | tf_op jit(solution)/shard_map/reduce_scatter | solution.py:225
  343.1 47.6 %copy-start.2 = (bf16[512,1024]{1,0:T(8,128)(2,1)S(1)}, bf16[512,1024]{1,0:T(8,128)(2,1)}, u32[]{:S(2)}) copy-start(bf16[512,1024]{1,0:T(8,128)(2,1)} %all-gather.13.cloned.1.call-done) | copy-start | bytes 3145732
  391.7 3.6 copy-start.8
  393.3 1.0 copy-start.5
  394.3 3.3 copy-start.4
  397.6 3.7 copy-start.1
  399.1 2.8 copy-start.3
  401.3 0.9 copy-start.9
Sparse Core Ops, SparseCore 0:
  9.6 19.4 all-gather.8
  30.6 16.7 all-gather.6
  48.9 16.7 all-gather.10
  87.7 227.9 all-gather.14
  317.2 14.9 all-gather.12
  335.1 31.4 reduce-scatter.1
